TPU v7x, 32 devices: a whole 2x2x4 slice. The times are simulated.
32 devices in a mesh: ma: 8 (over z, x), row: 4 (over y, core).
Axes of the slice: x: 2, y: 2, z: 4, core: 2. Of those that a mesh axis runs over, the one named last changes fastest.
Arguments:
- grid_field: bfloat16 [64, 1536, 512], P(None, 'ma', 'row'), may hold values from -6 to 6
- legendre: bfloat16 [64, 1024, 1536], P(('ma', 'row')), may hold values from -0.15625 to 0.15625
- order_table: int32 [64], P(('ma', 'row')), may hold values from 0 to 1023, as said below
- boundary_rows: int32 [2, 2], replicated, may hold values from 96 to 127, as said below
- inverse: bfloat16 [1024, 256, 256], P(('ma', 'row')), may hold values from -0.375 to 0.375
Outputs:
- spectra: bfloat16 [1024, 256, 128], P(('ma', 'row'))
Inputs may be any that keep to these rules, and one draw needn't show every extreme that they name: `order_table`: slots 2 i and 2 i + 1 hold the orders m and 1023 - m of one pair, m < 512 first; no order appears twice; the pair of 0 and 1023 is always present. `boundary_rows`: the four entries differ and lie in the top 128 // 4 Chebyshev rows; both ends of that range occur.
All inputs are finite; a program needn't handle non-finite values.
Results may differ from a plain program's by a relative error of at most 0.0049.
Values may be sent and summed in bfloat16 or wider, within the bound.
A program may use at most 192 MiB of HBM per device.

v0:
```python
import jax
import jax.numpy as jnp
from jax import lax
from jax.sharding import PartitionSpec as P

NR = 128


def chebyshev_table(radial_levels):
    wave_number = jnp.arange(radial_levels, dtype=jnp.float32)[:, None]
    grid_point = jnp.arange(radial_levels, dtype=jnp.float32)[None, :]
    cos_table = jnp.cos(jnp.pi * wave_number * (grid_point + 0.5) / radial_levels) * jnp.sqrt(
        2.0 / radial_levels
    )
    return jnp.where(wave_number == 0.0, cos_table * jnp.sqrt(0.5), cos_table)


def boundary_keep(boundary_rows, radial_levels):
    row_index = jnp.arange(radial_levels, dtype=jnp.int32)[None, :]
    boundary_hit = (row_index == boundary_rows[:, 0:1]) | (row_index == boundary_rows[:, 1:2])
    return jnp.where(boundary_hit, 0.0, 1.0).astype(jnp.float32)


def on_device(grid_field, legendre, order_table, boundary_rows, inverse):
    ma_count = lax.axis_size("ma")
    row_count = lax.axis_size("row")
    degree_total = legendre.shape[1]
    radial_levels = NR
    degree_share = degree_total // (ma_count * row_count)
    finished_output = lax.all_to_all(
        lax.all_to_all(grid_field, "ma", split_axis=0, concat_axis=1, tiled=True),
        "row",
        split_axis=0,
        concat_axis=2,
        tiled=True,
    )
    spectral_coefficients = jnp.einsum(
        "xso,xod->xsd", legendre, finished_output, preferred_element_type=jnp.float32
    )
    degrees = jnp.arange(degree_total, dtype=jnp.int32)
    lower_mask = degrees[None, :] >= order_table[:, None]
    spectral_coefficients = jnp.where(
        lower_mask[:, :, None], spectral_coefficients, jnp.zeros_like(spectral_coefficients)
    )
    chebyshev = chebyshev_table(radial_levels)
    keep_rows = boundary_keep(boundary_rows, radial_levels)
    regrouped = lax.all_to_all(
        lax.all_to_all(spectral_coefficients, "ma", split_axis=1, concat_axis=0, tiled=True),
        "row",
        split_axis=1,
        concat_axis=0,
        tiled=True,
    )
    regrouped = regrouped.reshape(row_count, ma_count, 2, degree_share, radial_levels, 2, 2)
    coefficients = jnp.einsum(
        "kj,bavljqp->lqkabvp", chebyshev, regrouped, precision=lax.Precision.HIGHEST
    )
    right_side = coefficients * keep_rows[None, :, :, None, None, None, None]
    right_side = right_side.reshape(degree_share, 2 * radial_levels, -1).astype(jnp.bfloat16)
    solved = jnp.einsum("lij,ljn->lin", inverse, right_side, preferred_element_type=jnp.float32)
    return solved.astype(jnp.bfloat16)


def solution(mesh):
    return jax.shard_map(
        on_device,
        mesh=mesh,
        in_specs=(
            P(None, "ma", "row"),
            P(("ma", "row"), None, None),
            P(("ma", "row")),
            P(),
            P(("ma", "row"), None, None),
        ),
        out_specs=P(("ma", "row"), None, None),
        check_vma=False,
    )
```

profile of v0, /device:TPU:29, one launch (start us, length us, event | category | flops | bytes accessed | tf_op | source)
XLA Modules:
  0.0 332.6 jit_solution(1943884224348974769)
XLA Ops:
  0.0 73.6 %all_to_all.69 = bf16[64,192,128]{2,1,0:T(8,128)(2,1)S(1)} all-to-all(bf16[64,192,128]{2,1,0:T(8,128)(2,1)} %param.5), channel_id=1, replica_groups=mesh['ma'=8,'row'=4] {'ma'}, dimensions={0} | all-to-all | bytes 6291456 | tf_op jit(solution)/shard_map/all_to_all | solution.py:31
  73.6 1.9 copy.28
  75.5 0.0 copy-start.1
  75.5 5.1 %all-to-all-start.1 = ((bf16[8,1536,128]{2,1,0:T(8,128)(2,1)}), bf16[8,1536,128]{2,1,0:T(8,128)(2,1)S(1)}, u32[]{:S(2)}, u32[]{:S(2)}) async-start(bf16[8,1536,128]{2,1,0:T(8,128)(2,1)} %bitcast.2), calls=%async_computation.1 | async-start | bytes 6291456 | tf_op jit(solution)/shard_map/all_to_all | solution.py:30
  80.6 0.0 copy-done.1
  80.6 0.1 iota_compare_fusion
  80.7 34.9 %all-to-all-done.1 = bf16[8,1536,128]{2,1,0:T(8,128)(2,1)S(1)} async-done(((bf16[8,1536,128]{2,1,0:T(8,128)(2,1)}), bf16[8,1536,128]{2,1,0:T(8,128)(2,1)S(1)}, u32[]{:S(2)}, u32[]{:S(2)}) %all-to-all-start.1) | async-done | bytes 3145760 | tf_op jit(solution)/shard_map/all_to_all | solution.py:30
  115.6 5.5 %broadcast_select_fusion = f32[2,1024,512]{2,1,0:T(8,128)S(1)} fusion(pred[2,1024]{1,0:T(4,128)(4,1)S(1)} %iota_compare_fusion, bf16[2,1024,1536]{2,1,0:T(8,128)(2,1)} %param.6, bf16[4,2,192,8,128]{4,3,2,1,0:T(8,128)(2,1)S(1)} %bitcast.39), kind=kOutput, calls=%fused_computation.8 | convolution fusion | flops 3222274048 | bytes 13633536 | tf_op jit(solution)/shard_map/xso,xod->xsd/dot_general | solution.py:37
  121.1 3.2 copy.30
  124.4 96.2 %all_to_all.70 = f32[2,1024,512]{2,0,1:T(2,128)S(1)} all-to-all(f32[2,1024,512]{2,0,1:T(2,128)S(1)} %copy.30), channel_id=1, replica_groups=mesh['ma'=8,'row'=4] {'ma'}, dimensions={1} | all-to-all | bytes 8388608 | tf_op jit(solution)/shard_map/all_to_all | solution.py:48
  220.5 0.8 copy.31
  221.3 0.6 copy.32
  221.9 4.4 %copy.33 = f32[16,128,512]{2,0,1:T(8,128)} copy(f32[16,128,512]{2,1,0:T(8,128)S(1)} %bitcast.37) | data formatting | bytes 8388608 | tf_op jit(solution)/shard_map/all_to_all | solution.py:48
  226.3 0.0 copy-start
  226.3 7.1 %all-to-all-start.3 = ((f32[16,128,512]{2,0,1:T(8,128)}), f32[16,128,512]{2,0,1:T(8,128)}, u32[]{:S(2)}, u32[]{:S(2)}) async-start(f32[16,128,512]{2,0,1:T(8,128)} %copy.33), calls=%async_computation.3 | async-start | bytes 8388608 | tf_op jit(solution)/shard_map/all_to_all | solution.py:47
  233.4 0.0 copy-done
  233.4 0.2 slice_reduce_fusion.1
  233.6 0.1 or_select_fusion
  233.6 46.0 %all-to-all-done.3 = f32[16,128,512]{2,0,1:T(8,128)} async-done(((f32[16,128,512]{2,0,1:T(8,128)}), f32[16,128,512]{2,0,1:T(8,128)}, u32[]{:S(2)}, u32[]{:S(2)}) %all-to-all-start.3) | async-done | bytes 4194336 | tf_op jit(solution)/shard_map/all_to_all | solution.py:47
  279.6 10.5 %copy.34 = f32[16,4,32,512]{2,3,0,1:T(8,128)} copy(f32[16,4,32,512]{3,0,2,1:T(8,128)} %bitcast.8) | data formatting | bytes 8388608 | tf_op jit(solution)/shard_map/all_to_all | solution.py:47
  290.2 30.4 %fusion.5 = bf16[32,2,128,8,4,2,2]{2,0,6,1,5,3,4:T(8,128)(2,1)S(1)} fusion(f32[2,128]{1,0:T(2,128)S(1)} %or_select_fusion, f32[4,8,2,32,128,2,2]{3,6,5,4,2,1,0:T(2,128)} %bitcast.35, f32[128]{0:T(128)S(1)} %get-tuple-element.7, f32[128]{0:T(128)S(1)} %get-tuple-element.8, pred[128]{0:T(512)(128)(4,1)S(1)} %iota_compare_fusion.1), kind=kOutput, calls=%fused_computation.6 | convolution fusion | flops 1612791808 | bytes 6293632 | tf_op jit(solution)/shard_map/kj,bavljqp->lqkabvp/dot_general | solution.py:55
  320.6 2.2 copy.36
  322.8 2.6 convert_element_type.17
  325.4 4.3 %convert_bitcast_fusion = bf16[32,256,128]{1,2,0:T(8,128)(2,1)S(1)} fusion(bf16[32,256,128]{1,2,0:T(8,128)(2,1)} %convert_element_type.17, bf16[32,256,256]{2,1,0:T(8,128)(2,1)} %param.9), kind=kOutput, calls=%fused_computation.7 | convolution fusion | flops 537919488 | bytes 8388608 | tf_op jit(solution)/shard_map/lij,ljn->lin/dot_general | solution.py:60
  329.7 2.9 copy.37
  (2 shorter events, 0.0 us)
Async XLA Ops:
  75.5 5.1 %copy-start.1 = (s32[2]{0:T(128)S(1)}, s32[2]{0:T(128)}, u32[]{:S(2)}) copy-start(s32[2]{0:T(128)} %param.7) | copy-start | bytes 28
  75.5 40.1 %all-to-all-start.1 = ((bf16[8,1536,128]{2,1,0:T(8,128)(2,1)}), bf16[8,1536,128]{2,1,0:T(8,128)(2,1)S(1)}, u32[]{:S(2)}, u32[]{:S(2)}) async-start(bf16[8,1536,128]{2,1,0:T(8,128)(2,1)} %bitcast.2), calls=%async_computation.1 | async-start | bytes 6291456 | tf_op jit(solution)/shard_map/all_to_all | solution.py:30
  226.3 7.1 %copy-start = (s32[2,2]{1,0:T(2,128)S(1)}, s32[2,2]{1,0:T(2,128)}, u32[]{:S(2)}) copy-start(s32[2,2]{1,0:T(2,128)} %param.8) | copy-start | bytes 52
  226.3 53.3 %all-to-all-start.3 = ((f32[16,128,512]{2,0,1:T(8,128)}), f32[16,128,512]{2,0,1:T(8,128)}, u32[]{:S(2)}, u32[]{:S(2)}) async-start(f32[16,128,512]{2,0,1:T(8,128)} %copy.33), calls=%async_computation.3 | async-start | bytes 8388608 | tf_op jit(solution)/shard_map/all_to_all | solution.py:47
where the time goes:
time: 339 us; the launch traced here: 333 us
  blocking collectives  170 us (50%)
  waiting for transfers between devices  80.9 us (24%)
  matrix products  40.3 us (12%)
  local copies, waits for them, and re-layouts  29.3 us (9%)
  starting transfers between devices  12.2 us (4%)
    all_to_all x1, blocking collectives, on_device(): lax.all_to_all(spectral_coefficients, 'ma', split_axis=1, concat_axis=0,...  96.2 us
    all_to_all x1, blocking collectives, on_device(): lax.all_to_all(grid_field, 'ma', split_axis=0, concat_axis=1, tiled=True)  73.6 us
    all_to_all x1, waiting for transfers between devices, on_device(): lax.all_to_all(lax.all_to_all(spectral_coefficients, 'ma', split_axis=1,...  46 us
    all_to_all x1, waiting for transfers between devices, on_device(): lax.all_to_all(lax.all_to_all(grid_field, 'ma', split_axis=0, concat_axis...  34.9 us
    dot_general x1, matrix products, on_device(): jnp.einsum('kj,bavljqp->lqkabvp', chebyshev, regrouped, precision=lax.Pre...  30.4 us
    all_to_all x1, local copies, waits for them, and re-layouts, on_device(): lax.all_to_all(lax.all_to_all(spectral_coefficients, 'ma', split_axis=1,...  10.5 us
    all_to_all x1, starting transfers between devices, on_device(): lax.all_to_all(lax.all_to_all(spectral_coefficients, 'ma', split_axis=1,...  7.06 us
  transfers between devices with their start and end apart: 2, of which 2 were waited for; matrix products, arithmetic and copies ran while one was open for 0% of the time, Pallas kernels for 0%

commit v1 on v0

v1 whole, which is shorter than its diff:
```python
import jax
import jax.numpy as jnp
from jax import lax
from jax.sharding import PartitionSpec as P


def chebyshev_table(radial_levels):
    wave_number = jnp.arange(radial_levels, dtype=jnp.float32)[:, None]
    grid_point = jnp.arange(radial_levels, dtype=jnp.float32)[None, :]
    cos_table = jnp.cos(jnp.pi * wave_number * (grid_point + 0.5) / radial_levels) * jnp.sqrt(
        2.0 / radial_levels
    )
    return jnp.where(wave_number == 0.0, cos_table * jnp.sqrt(0.5), cos_table)


def boundary_keep(boundary_rows, radial_levels):
    row_index = jnp.arange(radial_levels, dtype=jnp.int32)[None, :]
    boundary_hit = (row_index == boundary_rows[:, 0:1]) | (row_index == boundary_rows[:, 1:2])
    return jnp.where(boundary_hit, 0.0, 1.0).astype(jnp.float32)


def radial_matrix(boundary_rows, radial_levels):
    cheb = chebyshev_table(radial_levels)
    keep = boundary_keep(boundary_rows, radial_levels)
    eye = jnp.eye(2, dtype=jnp.float32)
    full = (
        cheb.T[:, None, None, None, None, :]
        * eye[None, :, None, None, :, None]
        * eye[None, None, :, :, None, None]
        * keep[None, None, None, None, :, :]
    )
    return full.reshape(4 * radial_levels, 4 * radial_levels)


def on_device(grid_field, legendre, order_table, boundary_rows, inverse):
    ma_count = lax.axis_size("ma")
    row_count = lax.axis_size("row")
    devices = ma_count * row_count
    slots, degree_total, latitudes = legendre.shape
    columns = grid_field.shape[2]
    radial_levels = columns * row_count // 4
    share = degree_total // devices
    got = lax.all_to_all(
        grid_field.reshape(devices, slots, latitudes // ma_count, columns),
        ("ma", "row"), split_axis=0, concat_axis=0, tiled=True,
    )
    got = got.reshape(ma_count, row_count, slots, latitudes // ma_count, columns)
    got = got.transpose(2, 0, 3, 1, 4).reshape(slots, latitudes, row_count * columns)
    spectrum = jnp.einsum("xlt,xtd->xld", legendre, got, preferred_element_type=jnp.float32)
    degrees = jnp.arange(degree_total, dtype=jnp.int32)
    lower = degrees[None, :] >= order_table[:, None]
    spectrum = jnp.where(lower[:, :, None], spectrum, 0.0)
    matrix = radial_matrix(boundary_rows, radial_levels)
    matrix_high = matrix.astype(jnp.bfloat16)
    matrix_low = (matrix - matrix_high.astype(jnp.float32)).astype(jnp.bfloat16)
    high = spectrum.astype(jnp.bfloat16)
    low = (spectrum - high.astype(jnp.float32)).astype(jnp.bfloat16)

    def mul(a, b):
        return jnp.einsum("xld,de->xle", a, b, preferred_element_type=jnp.float32)

    right = mul(high, matrix_high) + (mul(low, matrix_high) + mul(high, matrix_low))
    right = right.astype(jnp.bfloat16).reshape(slots, degree_total, 2, 2 * radial_levels)
    right = right.transpose(1, 0, 2, 3).reshape(devices, share, 2 * slots, 2 * radial_levels)
    right = lax.all_to_all(right, ("ma", "row"), split_axis=0, concat_axis=0, tiled=True)
    right = right.transpose(1, 0, 2, 3).reshape(share, devices * 2 * slots, 2 * radial_levels)
    solved = jnp.einsum("lij,lnj->lin", inverse, right, preferred_element_type=jnp.float32)
    return solved.astype(jnp.bfloat16)


def solution(mesh):
    return jax.shard_map(
        on_device,
        mesh=mesh,
        in_specs=(
            P(None, "ma", "row"),
            P(("ma", "row"), None, None),
            P(("ma", "row")),
            P(),
            P(("ma", "row"), None, None),
        ),
        out_specs=P(("ma", "row"), None, None),
        check_vma=False,
    )
```

time: 339 us -> 165 us (0.49)
  the two profiles are of different devices: /device:TPU:29 before, /device:TPU:0 now
where the time goes in v1:
time: 165 us; the launch traced here: 164 us
  waiting for transfers between devices  69.6 us (42%)
  blocking collectives  53 us (32%)
  local copies, waits for them, and re-layouts  20.3 us (12%)
  matrix products  13 us (8%)
  starting transfers between devices  7.41 us (4%)
    all_to_all x1, waiting for transfers between devices, on_device(): lax.all_to_all(grid_field.reshape(devices, slots, latitudes // ma_count,...  69.6 us
    all_to_all x1, blocking collectives, on_device(): lax.all_to_all(right, ('ma', 'row'), split_axis=0, concat_axis=0, tiled=T...  53 us
    all_to_all x1, starting transfers between devices, on_device(): lax.all_to_all(grid_field.reshape(devices, slots, latitudes // ma_count,...  7.41 us
    dot_general x1, matrix products, on_device(): jnp.einsum('xlt,xtd->xld', legendre, got, preferred_element_type=jnp.floa...  6.45 us
    transpose x1, local copies, waits for them, and re-layouts, on_device(): got.transpose(2, 0, 3, 1, 4).reshape(slots, latitudes, row_count * columns)  6.18 us
    reshape x1, local copies, waits for them, and re-layouts, on_device(): got.transpose(2, 0, 3, 1, 4).reshape(slots, latitudes, row_count * columns)  5.71 us
    dot_general x3, matrix products, mul(): return jnp.einsum('xld,de->xle', a, b, preferred_element_type=jnp.float32)  4.87 us
  transfers between devices with their start and end apart: 1, of which 1 were waited for; matrix products, arithmetic and copies ran while one was open for 1% of the time, Pallas kernels for 0%

profile of v1, /device:TPU:0, one launch (start us, length us, event | category | flops | bytes accessed | tf_op | source)
XLA Modules:
  0.0 164.5 jit_solution(8117558814495429891)
XLA Ops:
  0.0 0.0 copy-start.1
  0.0 0.0 copy-start.2
  0.0 7.4 %all-to-all-start = ((bf16[32,2,192,128]{3,2,1,0:T(8,128)(2,1)}), bf16[32,2,192,128]{3,2,1,0:T(8,128)(2,1)}, u32[]{:S(2)}, u32[]{:S(2)}) async-start(bf16[32,2,192,128]{3,2,1,0:T(8,128)(2,1)} %bitcast.28), calls=%async_computation | async-start | bytes 6291456 | tf_op jit(solution)/shard_map/all_to_all | solution.py:43
  7.5 0.3 multiply_select_fusion
  7.8 0.2 broadcast_multiply_fusion.1
  7.9 0.4 broadcast_multiply_fusion
  8.4 0.8 mul.114
  9.2 0.0 copy-done.1
  9.2 0.2 slice_reduce_fusion.1
  9.4 0.1 or_select_fusion
  9.5 0.0 copy-done.2
  9.5 0.1 iota_compare_fusion
  9.6 69.6 %all-to-all-done = bf16[32,2,192,128]{3,2,1,0:T(8,128)(2,1)} async-done(((bf16[32,2,192,128]{3,2,1,0:T(8,128)(2,1)}), bf16[32,2,192,128]{3,2,1,0:T(8,128)(2,1)}, u32[]{:S(2)}, u32[]{:S(2)}) %all-to-all-start) | async-done | bytes 3145760 | tf_op jit(solution)/shard_map/all_to_all | solution.py:43
  79.1 6.2 %copy.15 = bf16[2,8,192,4,128]{4,3,2,1,0:T(4,128)(2,1)} copy(bf16[2,8,192,4,128]{4,2,0,3,1:T(8,128)(2,1)} %bitcast.2) | data formatting | bytes 6291456 | tf_op jit(solution)/shard_map/transpose | solution.py:48
  85.3 5.7 %reshape.167 = bf16[2,1536,512]{2,1,0:T(8,128)(2,1)} reshape(bf16[2,8,192,4,128]{4,3,2,1,0:T(4,128)(2,1)} %copy.15) | data formatting | bytes 6291456 | tf_op jit(solution)/shard_map/reshape | solution.py:48
  91.0 6.4 %fusion.17 = f32[2,1024,512]{2,1,0:T(8,128)S(1)} fusion(bf16[2,1024,1536]{2,1,0:T(8,128)(2,1)} %param.6, bf16[2,1536,512]{2,1,0:T(8,128)(2,1)} %reshape.167), kind=kOutput, calls=%fused_computation.29 | convolution fusion | flops 3221225472 | bytes 13631488 | tf_op jit(solution)/shard_map/xlt,xtd->xld/dot_general | solution.py:49
  97.5 1.5 fusion
  99.0 1.5 fusion.7
  100.5 1.9 %add_convert_fusion = bf16[2,1024,512]{1,2,0:T(8,128)(2,1)S(1)} fusion(f32[2,1024,512]{1,2,0:T(8,128)S(1)} %fusion.7, f32[2,1024,512]{1,2,0:T(8,128)S(1)} %fusion, f32[2,1024,512]{2,1,0:T(8,128)S(1)} %fusion.17, pred[2,1024]{1,0:T(4,128)(4,1)S(1)} %iota_compare_fusion, f32[512,512]{1,0:T(8,128)S(1)} %mul.114, f32[512]{0:T(512)S(1)} %bitcast.31), kind=kOutput, calls=%fused_computation | convolution fusion | flops 1079246848 | bytes 15732736 | tf_op jit(solution)/shard_map/xld,de->xle/dot_general | solution.py:60
  102.4 2.6 %copy.19 = bf16[2,1024,2,256]{3,1,2,0:T(8,128)(2,1)} copy(bf16[2,1024,2,256]{1,3,2,0:T(8,128)(2,1)S(1)} %bitcast.25) | data formatting | bytes 4194304 | tf_op jit(solution)/shard_map/reshape | solution.py:63
  105.0 0.0 copy-start
  105.0 1.9 %copy.20 = bf16[32,32,4,256]{3,1,2,0:T(8,128)(2,1)S(1)} copy(bf16[32,32,4,256]{3,1,0,2:T(8,128)(2,1)} %bitcast.26) | data formatting | bytes 4194304 | tf_op jit(solution)/shard_map/reshape | solution.py:64
  106.9 53.0 %all_to_all.10 = bf16[32,32,4,256]{3,1,2,0:T(8,128)(2,1)S(1)} all-to-all(bf16[32,32,4,256]{3,1,2,0:T(8,128)(2,1)S(1)} %copy.20), channel_id=1, replica_groups=mesh['ma'=8,'row'=4] {'ma','row'}, dimensions={0} | all-to-all | bytes 4194304 | tf_op jit(solution)/shard_map/all_to_all | solution.py:65
  159.9 0.0 copy-done
  159.9 1.7 %convert_bitcast_fusion = bf16[32,256,128]{1,2,0:T(8,128)(2,1)S(1)} fusion(bf16[32,256,256]{2,1,0:T(8,128)(2,1)S(1)} %copy-done, bf16[32,128,256]{2,0,1:T(8,128)(2,1)S(1)} %bitcast.27), kind=kOutput, calls=%fused_computation.6 | convolution fusion | flops 537919488 | bytes 8388608 | tf_op jit(solution)/shard_map/lij,lnj->lin/dot_general | solution.py:67
  161.6 2.9 %copy.22 = bf16[32,256,128]{2,1,0:T(8,128)(2,1)} copy(bf16[32,256,128]{1,2,0:T(8,128)(2,1)S(1)} %convert_bitcast_fusion) | data formatting | bytes 4194304 | tf_op jit(solution)/shard_map/convert_element_type | solution.py:68
  (4 shorter events, 0.0 us)
Async XLA Ops:
  0.0 9.2 %copy-start.1 = (s32[2,2]{1,0:T(2,128)S(1)}, s32[2,2]{1,0:T(2,128)}, u32[]{:S(2)}) copy-start(s32[2,2]{1,0:T(2,128)} %param.8) | copy-start | bytes 52
  0.0 9.5 %copy-start.2 = (s32[2]{0:T(128)S(1)}, s32[2]{0:T(128)}, u32[]{:S(2)}) copy-start(s32[2]{0:T(128)} %param.7) | copy-start | bytes 28
  0.0 79.1 %all-to-all-start = ((bf16[32,2,192,128]{3,2,1,0:T(8,128)(2,1)}), bf16[32,2,192,128]{3,2,1,0:T(8,128)(2,1)}, u32[]{:S(2)}, u32[]{:S(2)}) async-start(bf16[32,2,192,128]{3,2,1,0:T(8,128)(2,1)} %bitcast.28), calls=%async_computation | async-start | bytes 6291456 | tf_op jit(solution)/shard_map/all_to_all | solution.py:43
  105.0 54.9 %copy-start = (bf16[32,256,256]{2,1,0:T(8,128)(2,1)S(1)}, bf16[32,256,256]{2,1,0:T(8,128)(2,1)}, u32[]{:S(2)}) copy-start(bf16[32,256,256]{2,1,0:T(8,128)(2,1)} %param.9) | copy-start | bytes 12582916

commit v2 on v1

--- a/solution.py
+++ b/solution.py
@@ -1,7 +1,16 @@
+import functools
+
 import jax
 import jax.numpy as jnp
+import numpy as np
 from jax import lax
+from jax.experimental import pallas as pl
+from jax.experimental.pallas import tpu as pltpu
 from jax.sharding import PartitionSpec as P
+
+MESH = pl.DeviceIdType.MESH
+GROUP = 8
+GROUPS = 4
 
 
 def chebyshev_table(radial_levels):
@@ -32,7 +41,7 @@
     return full.reshape(4 * radial_levels, 4 * radial_levels)
 
 
-def on_device(grid_field, legendre, order_table, boundary_rows, inverse):
+def with_collectives(grid_field, legendre, order_table, boundary_rows, inverse):
     ma_count = lax.axis_size("ma")
     row_count = lax.axis_size("row")
     devices = ma_count * row_count
@@ -66,6 +75,247 @@
     right = right.transpose(1, 0, 2, 3).reshape(share, devices * 2 * slots, 2 * radial_levels)
     solved = jnp.einsum("lij,lnj->lin", inverse, right, preferred_element_type=jnp.float32)
     return solved.astype(jnp.bfloat16)
+
+
+def radial_parts(radial_levels):
+    wave_number = np.arange(radial_levels, dtype=np.float64)[:, None]
+    point = np.arange(radial_levels, dtype=np.float64)[None, :] + 0.5
+    cheb = np.cos(np.pi * wave_number * point / radial_levels) * np.sqrt(2.0 / radial_levels)
+    cheb[0] *= np.sqrt(0.5)
+    full = np.zeros((radial_levels, 2, 2, 2, 2, radial_levels), np.float32)
+    for q in range(2):
+        for p in range(2):
+            full[:, q, p, p, q, :] = cheb.T
+    full = full.reshape(4 * radial_levels, 4 * radial_levels)
+    high = full.astype(jnp.bfloat16)
+    low = (full - high.astype(np.float32)).astype(jnp.bfloat16)
+    return np.stack([high, low])
+
+
+def kernel(
+    rows, order_ref, boundary_ref, grid_ref, legendre_ref, table_ref, inverse_ref, out_ref,
+    legendre, table, inverse, got, keep, send, landed, stage, solved,
+    load_sem, first_send, first_recv, second_send, second_recv, out_sem,
+):
+    slots, degrees, latitudes = legendre.shape
+    columns = grid_ref.shape[2]
+    band = grid_ref.shape[1]
+    devices = landed.shape[1]
+    share = landed.shape[2]
+    tile = GROUP * share
+    width = stage.shape[2]
+    orders = stage.shape[1] // share
+    ma = lax.axis_index("ma")
+    row = lax.axis_index("row")
+    me = ma * rows + row
+    z = me // GROUP
+    w = me % GROUP
+    z_order = (GROUPS - 1 - z, (z + GROUPS // 2) % GROUPS, z + 1 - 2 * (z % 2), z)
+
+    loads = [
+        pltpu.make_async_copy(legendre_ref, legendre, load_sem.at[0]),
+        pltpu.make_async_copy(table_ref, table, load_sem.at[1]),
+        pltpu.make_async_copy(inverse_ref, inverse, load_sem.at[2]),
+    ]
+    for load in loads:
+        load.start()
+
+    barrier = pltpu.get_barrier_semaphore()
+
+    @pl.loop(1, devices)
+    def _(k):
+        other = (me + k) % devices
+        pl.semaphore_signal(
+            barrier, inc=1, device_id=(other // rows, other % rows), device_id_type=MESH
+        )
+
+    pl.semaphore_wait(barrier, devices - 1)
+
+    def to_slots(slot):
+        here = got.at[
+            slot,
+            pl.ds(pl.multiple_of(ma * band, 16), band),
+            pl.ds(pl.multiple_of(row * columns, 128), columns),
+        ]
+
+        def send_to(other):
+            pltpu.make_async_remote_copy(
+                src_ref=grid_ref.at[other * slots + slot],
+                dst_ref=here,
+                send_sem=first_send.at[slot],
+                recv_sem=first_recv.at[slot],
+                device_id=(other // rows, other % rows),
+                device_id_type=MESH,
+            ).start()
+
+        for place, there in enumerate(z_order):
+            @pl.loop(0 if place < GROUPS - 1 else 1, GROUP)
+            def _(k, there=there):
+                send_to(there * GROUP + (w + k) % GROUP)
+
+        pltpu.make_async_copy(
+            grid_ref.at[me * slots + slot], here, first_recv.at[slot]
+        ).start()
+
+    for slot in range(slots):
+        to_slots(slot)
+
+    column = lax.broadcasted_iota(jnp.int32, keep.shape, 1)
+    mode = column % width
+    field = (column // width) % 2
+    first = jnp.where(field == 0, boundary_ref[0, 0], boundary_ref[1, 0])
+    last = jnp.where(field == 0, boundary_ref[0, 1], boundary_ref[1, 1])
+    keep[...] = jnp.where((mode == first) | (mode == last), 0.0, 1.0)
+
+    def analyse(slot, there):
+        start = pl.multiple_of(there * tile, tile)
+        spectrum = jnp.dot(
+            legendre[slot, pl.ds(start, tile), :], got[slot], preferred_element_type=jnp.float32
+        )
+        degree = start + lax.broadcasted_iota(jnp.int32, spectrum.shape, 0)
+        spectrum = jnp.where(degree >= order_ref[slot], spectrum, 0.0)
+        high = spectrum.astype(jnp.bfloat16)
+        low = (spectrum - high.astype(jnp.float32)).astype(jnp.bfloat16)
+        right = jnp.dot(high, table[0], preferred_element_type=jnp.float32)
+        right += jnp.dot(low, table[0], preferred_element_type=jnp.float32)
+        right += jnp.dot(high, table[1], preferred_element_type=jnp.float32)
+        right = jnp.where(keep[0:1, :] > 0.0, right, 0.0)
+        send[slot, pl.ds(start, tile), :] = right.astype(jnp.bfloat16)
+
+    def piece(slot, other):
+        return send.at[slot, pl.ds(pl.multiple_of(other * share, share), share)]
+
+    def to_degrees(slot, there, own):
+        @pl.loop(1 if own else 0, GROUP)
+        def _(k):
+            other = there * GROUP + (w + k) % GROUP
+            pltpu.make_async_remote_copy(
+                src_ref=piece(slot, other),
+                dst_ref=landed.at[slot, me],
+                send_sem=second_send.at[slot],
+                recv_sem=second_recv.at[slot],
+                device_id=(other // rows, other % rows),
+                device_id_type=MESH,
+            ).start()
+
+        if own:
+            pltpu.make_async_copy(
+                piece(slot, me), landed.at[slot, me], second_recv.at[slot]
+            ).start()
+
+    def wait_bytes(ref, sem):
+        pltpu.make_async_copy(ref, ref, sem).wait()
+
+    loads[0].wait()
+    loads[1].wait()
+    upper = z >= GROUPS // 2
+    wait_bytes(got.at[0], first_recv.at[0])
+    for place, there in enumerate(z_order):
+        analyse(0, there)
+        to_degrees(0, there, place == GROUPS - 1)
+    wait_bytes(got.at[1], first_recv.at[1])
+    for place, there in enumerate(z_order):
+        @pl.when(there >= GROUPS // 2)
+        def _(place=place, there=there):
+            analyse(1, there)
+            to_degrees(1, there, place == GROUPS - 1)
+
+    def put(slot, source, value):
+        for part in range(2):
+            for q in range(2):
+                at = (2 * part + q) * width
+                stage[
+                    q, pl.ds(source * 2 * slots + 2 * slot + part, share, stride=orders), :
+                ] = value[:, at:at + width]
+
+    def gather(slot):
+        @pl.loop(0, devices)
+        def _(source):
+            put(slot, source, landed[slot, source].astype(jnp.float32))
+
+    wait_bytes(landed.at[0], second_recv.at[0])
+    gather(0)
+
+    @pl.when(upper)
+    def _():
+        wait_bytes(landed.at[1], second_recv.at[1])
+        gather(1)
+
+    @pl.when(jnp.logical_not(upper))
+    def _():
+        @pl.loop(0, devices)
+        def _(source):
+            put(1, source, jnp.zeros((share, 4 * width), jnp.float32))
+
+    loads[2].wait()
+
+    @pl.loop(0, share)
+    def _(l):
+        at = pl.ds(pl.multiple_of(l * orders, orders), orders)
+        right = jnp.concatenate([stage[0, at, :], stage[1, at, :]], axis=1).astype(jnp.bfloat16)
+        solved[l] = lax.dot_general(
+            inverse[l], right, (((1,), (1,)), ((), ())), preferred_element_type=jnp.float32
+        ).astype(jnp.bfloat16)
+
+    result = pltpu.make_async_copy(solved, out_ref, out_sem)
+    result.start()
+    for slot in range(slots):
+        wait_bytes(grid_ref.at[pl.ds(0, devices - 1)], first_send.at[slot])
+    wait_bytes(send.at[0, pl.ds(0, (devices - 1) * share)], second_send.at[0])
+
+    @pl.when(upper)
+    def _():
+        wait_bytes(send.at[1, pl.ds(0, (devices // 2 - 1) * share)], second_send.at[1])
+
+    @pl.when(jnp.logical_not(upper))
+    def _():
+        wait_bytes(send.at[1, pl.ds(0, devices // 2 * share)], second_send.at[1])
+
+    result.wait()
+
+
+def on_device(grid_field, legendre, order_table, boundary_rows, inverse):
+    rows = lax.axis_size("row")
+    devices = lax.axis_size("ma") * rows
+    slots, degrees, latitudes = legendre.shape
+    band, columns = grid_field.shape[1:]
+    share = degrees // devices
+    full_width = columns * rows
+    orders = 2 * slots * devices
+    fits = (
+        devices == GROUP * GROUPS and slots == 2 and share % 16 == 0 and band % 16 == 0
+        and columns % 128 == 0 and full_width == 512
+    )
+    if not fits:
+        return with_collectives(grid_field, legendre, order_table, boundary_rows, inverse)
+    width = full_width // 4
+    any_space = pl.BlockSpec(memory_space=pl.ANY)
+    scalars = pl.BlockSpec(memory_space=pltpu.SMEM)
+    dma = pltpu.SemaphoreType.DMA
+    return pl.pallas_call(
+        functools.partial(kernel, rows),
+        out_shape=jax.ShapeDtypeStruct((share, 2 * width, orders), jnp.bfloat16),
+        in_specs=[scalars, scalars, any_space, any_space, any_space, any_space],
+        out_specs=any_space,
+        scratch_shapes=[
+            pltpu.VMEM(legendre.shape, jnp.bfloat16),
+            pltpu.VMEM((2, full_width, full_width), jnp.bfloat16),
+            pltpu.VMEM(inverse.shape, jnp.bfloat16),
+            pltpu.VMEM((slots, latitudes, full_width), jnp.bfloat16),
+            pltpu.VMEM((8, full_width), jnp.float32),
+            pltpu.VMEM((slots, degrees, full_width), jnp.bfloat16),
+            pltpu.VMEM((slots, devices, share, full_width), jnp.bfloat16),
+            pltpu.VMEM((2, share * orders, width), jnp.float32),
+            pltpu.VMEM((share, 2 * width, orders), jnp.bfloat16),
+            dma((3,)), dma((slots,)), dma((slots,)), dma((slots,)), dma((slots,)), dma,
+        ],
+        compiler_params=pltpu.CompilerParams(
+            collective_id=0, has_side_effects=True, vmem_limit_bytes=44 * 2 ** 20
+        ),
+        cost_estimate=pl.CostEstimate(
+            flops=6 * 10 ** 9, bytes_accessed=18 * 2 ** 20, transcendentals=0
+        ),
+    )(order_table, boundary_rows, grid_field, legendre, radial_parts(width), inverse)
 
 
 def solution(mesh):

time: 165 us -> 135 us (0.82)
  the two profiles are of different devices: /device:TPU:0 before, /device:TPU:29 now
where the time goes in v2:
time: 135 us
  Pallas kernels  129 us (96%)
  local copies, waits for them, and re-layouts  5.77 us (4%)
    pallas_call x1, Pallas kernels, on_device(): pl.pallas_call(functools.partial(kernel, rows), out_shape=jax.ShapeDtypeS...  129 us
    unnamed x9, local copies, waits for them, and re-layouts  5.77 us

profile of v2, /device:TPU:29, one launch (start us, length us, event | category | flops | bytes accessed | tf_op | source)
XLA Modules:
  0.0 134.9 jit_solution(10155343377882802600)
XLA Ops:
  0.0 0.0 copy-start
  0.0 1.9 %copy-done = bf16[64,192,128]{2,1,0:T(8,128)(2,1)S(1)} copy-done((bf16[64,192,128]{2,1,0:T(8,128)(2,1)S(1)}, bf16[64,192,128]{2,1,0:T(8,128)(2,1)}, u32[]{:S(2)}) %copy-start) | copy-done | bytes 3145752
  1.9 0.0 copy-start.1
  1.9 0.7 copy-done.1
  2.6 0.0 copy-start.2
  2.6 0.7 copy-done.2
  3.2 0.0 copy-start.3
  3.2 1.2 copy-done.3
  4.5 129.1 %shard_map.64 = bf16[32,256,128]{2,1,0:T(8,128)(2,1)S(1)} custom-call(s32[2]{0:T(128)S(1)} %copy-done.2, s32[2,2]{1,0:T(2,128)S(1)} %copy-done.1, bf16[64,192,128]{2,1,0:T(8,128)(2,1)S(1)} %copy-done, bf16[2,1024,1536]{2,1,0:T(8,128)(2,1)} %legendre_ref.1, bf16[2,512,512]{2,1,0:T(8,128)(2,1)S(1)} %copy-done.3, bf16[32,256,256]{2,1,0:T(8,128)(2,1)} %inverse_ref.1), custom_call_target="tpu_custom_call" | custom-call | flops 6000000000 | bytes 18874368 | tf_op jit(solution)/shard_map/pallas_call | solution.py:295
  133.6 1.3 copy.8
Async XLA Ops:
  0.0 1.9 %copy-start = (bf16[64,192,128]{2,1,0:T(8,128)(2,1)S(1)}, bf16[64,192,128]{2,1,0:T(8,128)(2,1)}, u32[]{:S(2)}) copy-start(bf16[64,192,128]{2,1,0:T(8,128)(2,1)} %grid_ref.1) | copy-start | bytes 9437188
  1.9 0.7 copy-start.1
  2.6 0.7 copy-start.2
  3.2 1.2 copy-start.3

commit v3 on v2

--- a/solution.py
+++ b/solution.py
@@ -87,13 +87,12 @@
         for p in range(2):
             full[:, q, p, p, q, :] = cheb.T
     full = full.reshape(4 * radial_levels, 4 * radial_levels)
-    high = full.astype(jnp.bfloat16)
-    low = (full - high.astype(np.float32)).astype(jnp.bfloat16)
-    return np.stack([high, low])
+    return full
 
 
 def kernel(
-    rows, order_ref, boundary_ref, grid_ref, legendre_ref, table_ref, inverse_ref, out_ref,
+    rows, order_hbm, boundary_hbm, grid_ref, legendre_ref, table_hbm, inverse_ref, out_ref,
+    order_ref, boundary_ref, table_ref,
     legendre, table, inverse, got, keep, send, landed, stage, solved,
     load_sem, first_send, first_recv, second_send, second_recv, out_sem,
 ):
@@ -111,11 +110,14 @@
     z = me // GROUP
     w = me % GROUP
     z_order = (GROUPS - 1 - z, (z + GROUPS // 2) % GROUPS, z + 1 - 2 * (z % 2), z)
+    z_mixed = (z_order[0], z_order[2], z_order[1], z_order[3])
 
     loads = [
         pltpu.make_async_copy(legendre_ref, legendre, load_sem.at[0]),
-        pltpu.make_async_copy(table_ref, table, load_sem.at[1]),
+        pltpu.make_async_copy(table_hbm, table_ref, load_sem.at[1]),
         pltpu.make_async_copy(inverse_ref, inverse, load_sem.at[2]),
+        pltpu.make_async_copy(order_hbm, order_ref, load_sem.at[3]),
+        pltpu.make_async_copy(boundary_hbm, boundary_ref, load_sem.at[4]),
     ]
     for load in loads:
         load.start()
@@ -148,10 +150,13 @@
                 device_id_type=MESH,
             ).start()
 
-        for place, there in enumerate(z_order):
-            @pl.loop(0 if place < GROUPS - 1 else 1, GROUP)
-            def _(k, there=there):
+        @pl.loop(1, GROUP)
+        def _(k):
+            for there in z_mixed:
                 send_to(there * GROUP + (w + k) % GROUP)
+
+        for there in z_mixed[:-1]:
+            send_to(there * GROUP + w)
 
         pltpu.make_async_copy(
             grid_ref.at[me * slots + slot], here, first_recv.at[slot]
@@ -160,6 +165,11 @@
     for slot in range(slots):
         to_slots(slot)
 
+    for load in loads[1:]:
+        load.wait()
+    full = table_ref[...]
+    table[0] = full.astype(jnp.bfloat16)
+    table[1] = (full - table[0].astype(jnp.float32)).astype(jnp.bfloat16)
     column = lax.broadcasted_iota(jnp.int32, keep.shape, 1)
     mode = column % width
     field = (column // width) % 2
@@ -185,40 +195,51 @@
     def piece(slot, other):
         return send.at[slot, pl.ds(pl.multiple_of(other * share, share), share)]
 
-    def to_degrees(slot, there, own):
-        @pl.loop(1 if own else 0, GROUP)
-        def _(k):
-            other = there * GROUP + (w + k) % GROUP
-            pltpu.make_async_remote_copy(
-                src_ref=piece(slot, other),
-                dst_ref=landed.at[slot, me],
-                send_sem=second_send.at[slot],
-                recv_sem=second_recv.at[slot],
-                device_id=(other // rows, other % rows),
-                device_id_type=MESH,
-            ).start()
-
-        if own:
-            pltpu.make_async_copy(
-                piece(slot, me), landed.at[slot, me], second_recv.at[slot]
-            ).start()
+    def to_degree(slot, other):
+        pltpu.make_async_remote_copy(
+            src_ref=piece(slot, other),
+            dst_ref=landed.at[slot, me],
+            send_sem=second_send.at[slot],
+            recv_sem=second_recv.at[slot, z],
+            device_id=(other // rows, other % rows),
+            device_id_type=MESH,
+        ).start()
+
+    def keep_own(slot):
+        pltpu.make_async_copy(
+            piece(slot, me), landed.at[slot, me], second_recv.at[slot, z]
+        ).start()
 
     def wait_bytes(ref, sem):
         pltpu.make_async_copy(ref, ref, sem).wait()
 
     loads[0].wait()
-    loads[1].wait()
     upper = z >= GROUPS // 2
     wait_bytes(got.at[0], first_recv.at[0])
-    for place, there in enumerate(z_order):
+    for there in z_order:
         analyse(0, there)
-        to_degrees(0, there, place == GROUPS - 1)
+
+    @pl.loop(1, GROUP)
+    def _(k):
+        for there in z_mixed:
+            to_degree(0, there * GROUP + (w + k) % GROUP)
+
+    for there in z_mixed[:-1]:
+        to_degree(0, there * GROUP + w)
+    keep_own(0)
     wait_bytes(got.at[1], first_recv.at[1])
     for place, there in enumerate(z_order):
         @pl.when(there >= GROUPS // 2)
         def _(place=place, there=there):
+            own = place == GROUPS - 1
             analyse(1, there)
-            to_degrees(1, there, place == GROUPS - 1)
+
+            @pl.loop(1 if own else 0, GROUP)
+            def _(k):
+                to_degree(1, there * GROUP + (w + k) % GROUP)
+
+            if own:
+                keep_own(1)
 
     def put(slot, source, value):
         for part in range(2):
@@ -229,17 +250,14 @@
                 ] = value[:, at:at + width]
 
     def gather(slot):
-        @pl.loop(0, devices)
-        def _(source):
-            put(slot, source, landed[slot, source].astype(jnp.float32))
-
-    wait_bytes(landed.at[0], second_recv.at[0])
-    gather(0)
-
-    @pl.when(upper)
-    def _():
-        wait_bytes(landed.at[1], second_recv.at[1])
-        gather(1)
+        for source_z in z_order[::-1]:
+            part = pl.ds(source_z * GROUP, GROUP)
+            wait_bytes(landed.at[slot, part], second_recv.at[slot, source_z])
+
+            @pl.loop(0, GROUP)
+            def _(k):
+                source = source_z * GROUP + k
+                put(slot, source, landed[slot, source].astype(jnp.float32))
 
     @pl.when(jnp.logical_not(upper))
     def _():
@@ -247,18 +265,29 @@
         def _(source):
             put(1, source, jnp.zeros((share, 4 * width), jnp.float32))
 
-    loads[2].wait()
-
-    @pl.loop(0, share)
-    def _(l):
-        at = pl.ds(pl.multiple_of(l * orders, orders), orders)
-        right = jnp.concatenate([stage[0, at, :], stage[1, at, :]], axis=1).astype(jnp.bfloat16)
-        solved[l] = lax.dot_general(
-            inverse[l], right, (((1,), (1,)), ((), ())), preferred_element_type=jnp.float32
-        ).astype(jnp.bfloat16)
-
-    result = pltpu.make_async_copy(solved, out_ref, out_sem)
-    result.start()
+    gather(0)
+
+    @pl.when(upper)
+    def _():
+        gather(1)
+
+    some = share // 4
+
+    @pl.loop(0, 4)
+    def _(step):
+        @pl.loop(0, some, unroll=4)
+        def _(k):
+            l = step * some + k
+            at = pl.ds(pl.multiple_of(l * orders, orders), orders)
+            right = jnp.concatenate([stage[0, at, :], stage[1, at, :]], axis=1)
+            solved[l] = lax.dot_general(
+                inverse[l], right.astype(jnp.bfloat16), (((1,), (1,)), ((), ())),
+                preferred_element_type=jnp.float32,
+            ).astype(jnp.bfloat16)
+
+        done = pl.ds(step * some, some)
+        pltpu.make_async_copy(solved.at[done], out_ref.at[done], out_sem).start()
+
     for slot in range(slots):
         wait_bytes(grid_ref.at[pl.ds(0, devices - 1)], first_send.at[slot])
     wait_bytes(send.at[0, pl.ds(0, (devices - 1) * share)], second_send.at[0])
@@ -271,7 +300,7 @@
     def _():
         wait_bytes(send.at[1, pl.ds(0, devices // 2 * share)], second_send.at[1])
 
-    result.wait()
+    wait_bytes(solved, out_sem)
 
 
 def on_device(grid_field, legendre, order_table, boundary_rows, inverse):
@@ -290,14 +319,16 @@
         return with_collectives(grid_field, legendre, order_table, boundary_rows, inverse)
     width = full_width // 4
     any_space = pl.BlockSpec(memory_space=pl.ANY)
-    scalars = pl.BlockSpec(memory_space=pltpu.SMEM)
     dma = pltpu.SemaphoreType.DMA
     return pl.pallas_call(
         functools.partial(kernel, rows),
         out_shape=jax.ShapeDtypeStruct((share, 2 * width, orders), jnp.bfloat16),
-        in_specs=[scalars, scalars, any_space, any_space, any_space, any_space],
+        in_specs=[any_space] * 6,
         out_specs=any_space,
         scratch_shapes=[
+            pltpu.SMEM(order_table.shape, jnp.int32),
+            pltpu.SMEM(boundary_rows.shape, jnp.int32),
+            pltpu.VMEM((full_width, full_width), jnp.float32),
             pltpu.VMEM(legendre.shape, jnp.bfloat16),
             pltpu.VMEM((2, full_width, full_width), jnp.bfloat16),
             pltpu.VMEM(inverse.shape, jnp.bfloat16),
@@ -307,10 +338,10 @@
             pltpu.VMEM((slots, devices, share, full_width), jnp.bfloat16),
             pltpu.VMEM((2, share * orders, width), jnp.float32),
             pltpu.VMEM((share, 2 * width, orders), jnp.bfloat16),
-            dma((3,)), dma((slots,)), dma((slots,)), dma((slots,)), dma((slots,)), dma,
+            dma((5,)), dma((slots,)), dma((slots,)), dma((slots,)), dma((slots, GROUPS)), dma,
         ],
         compiler_params=pltpu.CompilerParams(
-            collective_id=0, has_side_effects=True, vmem_limit_bytes=44 * 2 ** 20
+            collective_id=0, has_side_effects=True, vmem_limit_bytes=60 * 2 ** 20
         ),
         cost_estimate=pl.CostEstimate(
             flops=6 * 10 ** 9, bytes_accessed=18 * 2 ** 20, transcendentals=0

time: 135 us -> 127 us (0.941)
  Pallas kernels: 129 us -> 123 us
  local copies, waits for them, and re-layouts: 5.77 us -> 3.14 us
    pallas_call x1, Pallas kernels: 129 us -> 123 us  [on_device(): pl.pallas_call(functools.partial(kernel, rows), out_shape=jax.ShapeDtypeS...]
    unnamed x9 -> x1, local copies, waits for them, and re-layouts: 5.77 us -> 3.14 us
where the time goes in v3:
time: 127 us
  Pallas kernels  123 us (97%)
  local copies, waits for them, and re-layouts  3.14 us (2%)
    pallas_call x1, Pallas kernels, on_device(): pl.pallas_call(functools.partial(kernel, rows), out_shape=jax.ShapeDtypeS...  123 us
    unnamed x1, local copies, waits for them, and re-layouts  3.14 us

profile of v3, /device:TPU:29, one launch (start us, length us, event | category | flops | bytes accessed | tf_op | source)
XLA Modules:
  0.0 126.6 jit_solution(6973925918169183106)
XLA Ops:
  0.0 123.4 %shard_map.64 = bf16[32,256,128]{2,1,0:T(8,128)(2,1)} custom-call(s32[2]{0:T(128)} %order_hbm.1, s32[2,2]{1,0:T(2,128)} %boundary_hbm.1, bf16[64,192,128]{2,1,0:T(8,128)(2,1)} %grid_ref.1, bf16[2,1024,1536]{2,1,0:T(8,128)(2,1)} %legendre_ref.1, f32[512,512]{1,0:T(8,128)} %constant.2.clone.table_hbm, bf16[32,256,256]{2,1,0:T(8,128)(2,1)} %inverse_ref.1), custom_call_target="tpu_custom_call" | custom-call | flops 6000000000 | bytes 18874368 | tf_op jit(solution)/shard_map/pallas_call | solution.py:323
  123.4 3.1 %copy.8 = bf16[32,256,128]{2,1,0:T(8,128)(2,1)} copy(bf16[32,256,128]{2,1,0:T(8,128)(2,1)} %shard_map.64) | data formatting | bytes 4194304

commit v4 on v3

--- a/solution.py
+++ b/solution.py
@@ -134,11 +134,7 @@
     pl.semaphore_wait(barrier, devices - 1)
 
     def to_slots(slot):
-        here = got.at[
-            slot,
-            pl.ds(pl.multiple_of(ma * band, 16), band),
-            pl.ds(pl.multiple_of(row * columns, 128), columns),
-        ]
+        here = got.at[slot, row, pl.ds(pl.multiple_of(ma * band, 16), band)]
 
         def send_to(other):
             pltpu.make_async_remote_copy(
@@ -179,8 +175,9 @@
 
     def analyse(slot, there):
         start = pl.multiple_of(there * tile, tile)
+        grid = jnp.concatenate([got[slot, band_row] for band_row in range(rows)], axis=1)
         spectrum = jnp.dot(
-            legendre[slot, pl.ds(start, tile), :], got[slot], preferred_element_type=jnp.float32
+            legendre[slot, pl.ds(start, tile), :], grid, preferred_element_type=jnp.float32
         )
         degree = start + lax.broadcasted_iota(jnp.int32, spectrum.shape, 0)
         spectrum = jnp.where(degree >= order_ref[slot], spectrum, 0.0)
@@ -192,23 +189,29 @@
         right = jnp.where(keep[0:1, :] > 0.0, right, 0.0)
         send[slot, pl.ds(start, tile), :] = right.astype(jnp.bfloat16)
 
-    def piece(slot, other):
-        return send.at[slot, pl.ds(pl.multiple_of(other * share, share), share)]
-
-    def to_degree(slot, other):
+    def piece(slot, other, at, count):
+        return send.at[slot, pl.ds(pl.multiple_of(other * share + at, 16), count)]
+
+    def to_degree(slot, other, half):
+        at, count = (0, share) if half is None else (half * (share // 2), share // 2)
+        sem = second_recv.at[slot, half or 0, z]
+        here = landed.at[slot, me, pl.ds(at, count)]
+        return piece(slot, other, at, count), here, sem
+
+    def copy_to(slot, other, half=None):
+        source, here, sem = to_degree(slot, other, half)
         pltpu.make_async_remote_copy(
-            src_ref=piece(slot, other),
-            dst_ref=landed.at[slot, me],
+            src_ref=source,
+            dst_ref=here,
             send_sem=second_send.at[slot],
-            recv_sem=second_recv.at[slot, z],
+            recv_sem=sem,
             device_id=(other // rows, other % rows),
             device_id_type=MESH,
         ).start()
 
-    def keep_own(slot):
-        pltpu.make_async_copy(
-            piece(slot, me), landed.at[slot, me], second_recv.at[slot, z]
-        ).start()
+    def keep_own(slot, half=None):
+        source, here, sem = to_degree(slot, me, half)
+        pltpu.make_async_copy(source, here, sem).start()
 
     def wait_bytes(ref, sem):
         pltpu.make_async_copy(ref, ref, sem).wait()
@@ -216,67 +219,86 @@
     loads[0].wait()
     upper = z >= GROUPS // 2
     wait_bytes(got.at[0], first_recv.at[0])
-    for there in z_order:
-        analyse(0, there)
+    far, near, next_far, own = z_mixed
+    analyse(0, far)
+
+    @pl.loop(0, GROUP)
+    def _(k):
+        copy_to(0, far * GROUP + (w + k) % GROUP)
+
+    analyse(0, next_far)
+    analyse(0, near)
+
+    @pl.loop(0, GROUP)
+    def _(k):
+        for there in (next_far, near):
+            copy_to(0, there * GROUP + (w + k) % GROUP)
+
+    analyse(0, own)
 
     @pl.loop(1, GROUP)
     def _(k):
-        for there in z_mixed:
-            to_degree(0, there * GROUP + (w + k) % GROUP)
-
-    for there in z_mixed[:-1]:
-        to_degree(0, there * GROUP + w)
+        copy_to(0, own * GROUP + (w + k) % GROUP)
+
     keep_own(0)
     wait_bytes(got.at[1], first_recv.at[1])
-    for place, there in enumerate(z_order):
-        @pl.when(there >= GROUPS // 2)
-        def _(place=place, there=there):
-            own = place == GROUPS - 1
-            analyse(1, there)
-
-            @pl.loop(1 if own else 0, GROUP)
-            def _(k):
-                to_degree(1, there * GROUP + (w + k) % GROUP)
-
-            if own:
-                keep_own(1)
-
-    def put(slot, source, value):
+    up = z // (GROUPS // 2)
+    one = far + up * (near - far)
+    two = next_far + up * (own - next_far)
+
+    def copy_half(there, skip, half):
+        @pl.loop(skip, GROUP)
+        def _(k):
+            copy_to(1, there * GROUP + (w + k) % GROUP, half)
+
+    analyse(1, one)
+    copy_half(one, 0, 0)
+    analyse(1, two)
+    copy_half(two, up, 0)
+    copy_half(one, 0, 1)
+    copy_half(two, up, 1)
+
+    @pl.when(upper)
+    def _():
+        keep_own(1, 0)
+        keep_own(1, 1)
+
+    def put(slot, source, at, value):
         for part in range(2):
             for q in range(2):
-                at = (2 * part + q) * width
-                stage[
-                    q, pl.ds(source * 2 * slots + 2 * slot + part, share, stride=orders), :
-                ] = value[:, at:at + width]
-
-    def gather(slot):
+                first_row = at * orders + source * 2 * slots + 2 * slot + part
+                column = (2 * part + q) * width
+                stage[q, pl.ds(first_row, value.shape[0], stride=orders), :] = value[
+                    :, column:column + width
+                ]
+
+    def gather(slot, half=None):
+        at, count = (0, share) if half is None else (half * (share // 2), share // 2)
         for source_z in z_order[::-1]:
-            part = pl.ds(source_z * GROUP, GROUP)
-            wait_bytes(landed.at[slot, part], second_recv.at[slot, source_z])
+            part = landed.at[slot, pl.ds(source_z * GROUP, GROUP), pl.ds(at, count)]
+            wait_bytes(part, second_recv.at[slot, half or 0, source_z])
 
             @pl.loop(0, GROUP)
             def _(k):
                 source = source_z * GROUP + k
-                put(slot, source, landed[slot, source].astype(jnp.float32))
+                put(slot, source, at, landed[slot, source, at:at + count].astype(jnp.float32))
 
     @pl.when(jnp.logical_not(upper))
     def _():
         @pl.loop(0, devices)
         def _(source):
-            put(1, source, jnp.zeros((share, 4 * width), jnp.float32))
+            put(1, source, 0, jnp.zeros((share, 4 * width), jnp.float32))
 
     gather(0)
-
-    @pl.when(upper)
-    def _():
-        gather(1)
-
     some = share // 4
-
-    @pl.loop(0, 4)
-    def _(step):
+    for step in range(4):
+        if step % 2 == 0:
+            @pl.when(upper)
+            def _(step=step):
+                gather(1, step // 2)
+
         @pl.loop(0, some, unroll=4)
-        def _(k):
+        def _(k, step=step):
             l = step * some + k
             at = pl.ds(pl.multiple_of(l * orders, orders), orders)
             right = jnp.concatenate([stage[0, at, :], stage[1, at, :]], axis=1)
@@ -312,7 +334,7 @@
     full_width = columns * rows
     orders = 2 * slots * devices
     fits = (
-        devices == GROUP * GROUPS and slots == 2 and share % 16 == 0 and band % 16 == 0
+        devices == GROUP * GROUPS and slots == 2 and share % 32 == 0 and band % 16 == 0
         and columns % 128 == 0 and full_width == 512
     )
     if not fits:
@@ -320,10 +342,14 @@
     width = full_width // 4
     any_space = pl.BlockSpec(memory_space=pl.ANY)
     dma = pltpu.SemaphoreType.DMA
+    operands = (
+        order_table, boundary_rows, grid_field, legendre, jnp.asarray(radial_parts(width)), inverse
+    )
+    operands = [pltpu.with_memory_space_constraint(each, pltpu.HBM) for each in operands]
     return pl.pallas_call(
         functools.partial(kernel, rows),
         out_shape=jax.ShapeDtypeStruct((share, 2 * width, orders), jnp.bfloat16),
-        in_specs=[any_space] * 6,
+        in_specs=[pl.BlockSpec(memory_space=pltpu.HBM)] * 6,
         out_specs=any_space,
         scratch_shapes=[
             pltpu.SMEM(order_table.shape, jnp.int32),
@@ -332,21 +358,21 @@
             pltpu.VMEM(legendre.shape, jnp.bfloat16),
             pltpu.VMEM((2, full_width, full_width), jnp.bfloat16),
             pltpu.VMEM(inverse.shape, jnp.bfloat16),
-            pltpu.VMEM((slots, latitudes, full_width), jnp.bfloat16),
+            pltpu.VMEM((slots, rows, latitudes, columns), jnp.bfloat16),
             pltpu.VMEM((8, full_width), jnp.float32),
             pltpu.VMEM((slots, degrees, full_width), jnp.bfloat16),
             pltpu.VMEM((slots, devices, share, full_width), jnp.bfloat16),
             pltpu.VMEM((2, share * orders, width), jnp.float32),
             pltpu.VMEM((share, 2 * width, orders), jnp.bfloat16),
-            dma((5,)), dma((slots,)), dma((slots,)), dma((slots,)), dma((slots, GROUPS)), dma,
+            dma((5,)), dma((slots,)), dma((slots,)), dma((slots,)), dma((slots, 2, GROUPS)), dma,
         ],
         compiler_params=pltpu.CompilerParams(
-            collective_id=0, has_side_effects=True, vmem_limit_bytes=60 * 2 ** 20
+            collective_id=0, has_side_effects=True, vmem_limit_bytes=44 * 2 ** 20
         ),
         cost_estimate=pl.CostEstimate(
             flops=6 * 10 ** 9, bytes_accessed=18 * 2 ** 20, transcendentals=0
         ),
-    )(order_table, boundary_rows, grid_field, legendre, radial_parts(width), inverse)
+    )(*operands)
 
 
 def solution(mesh):

time: 127 us -> 123 us (0.969)
  Pallas kernels: 123 us -> 121 us
  local copies, waits for them, and re-layouts: 3.14 us -> 1.32 us
    pallas_call x1, Pallas kernels: 123 us -> 121 us  [on_device(): pl.pallas_call(functools.partial(kernel, rows), out_shape=jax.ShapeDtypeS...]
    unnamed x1, local copies, waits for them, and re-layouts: 3.14 us -> 1.32 us
where the time goes in v4:
time: 123 us; the launch traced here: 122 us
  Pallas kernels  121 us (98%)
  local copies, waits for them, and re-layouts  1.32 us (1%)
    pallas_call x1, Pallas kernels, on_device(): pl.pallas_call(functools.partial(kernel, rows), out_shape=jax.ShapeDtypeS...  121 us

profile of v4, /device:TPU:29, one launch (start us, length us, event | category | flops | bytes accessed | tf_op | source)
XLA Modules:
  0.0 122.5 jit_solution(2477232471785696662)
XLA Ops:
  0.0 121.2 %shard_map.64 = bf16[32,256,128]{2,1,0:T(8,128)(2,1)S(1)} custom-call(s32[2]{0:T(128)} %order_hbm.1, s32[2,2]{1,0:T(2,128)} %boundary_hbm.1, bf16[64,192,128]{2,1,0:T(8,128)(2,1)} %grid_ref.1, bf16[2,1024,1536]{2,1,0:T(8,128)(2,1)} %legendre_ref.1, f32[512,512]{1,0:T(8,128)} %constant.2.clone.table_hbm, bf16[32,256,256]{2,1,0:T(8,128)(2,1)} %inverse_ref.1), custom_call_target="tpu_custom_call" | custom-call | flops 6000000000 | bytes 18874368 | tf_op jit(solution)/shard_map/pallas_call | solution.py:349
  121.2 1.3 %copy.8 = bf16[32,256,128]{2,1,0:T(8,128)(2,1)} copy(bf16[32,256,128]{2,1,0:T(8,128)(2,1)S(1)} %shard_map.64) | data formatting | bytes 4194304

commit v5 on v4

--- a/solution.py
+++ b/solution.py
@@ -110,7 +110,12 @@
     z = me // GROUP
     w = me % GROUP
     z_order = (GROUPS - 1 - z, (z + GROUPS // 2) % GROUPS, z + 1 - 2 * (z % 2), z)
-    z_mixed = (z_order[0], z_order[2], z_order[1], z_order[3])
+    inner = z * (GROUPS - 1 - z) // 2
+    outer = 1 - inner
+    turns = tuple(
+        z_order[place] + inner * (z_order[(place + 2) % 4] - z_order[place]) for place in range(4)
+    )
+    skips = (0, inner, 0, outer)
 
     loads = [
         pltpu.make_async_copy(legendre_ref, legendre, load_sem.at[0]),
@@ -146,13 +151,17 @@
                 device_id_type=MESH,
             ).start()
 
-        @pl.loop(1, GROUP)
-        def _(k):
-            for there in z_mixed:
-                send_to(there * GROUP + (w + k) % GROUP)
-
-        for there in z_mixed[:-1]:
-            send_to(there * GROUP + w)
+        for pair in range(0, 4, 2):
+            @pl.loop(1, GROUP)
+            def _(k, pair=pair):
+                for there in turns[pair:pair + 2]:
+                    send_to(there * GROUP + (w + k) % GROUP)
+
+            send_to(turns[pair] * GROUP + w)
+
+            @pl.loop(skips[pair + 1], 1)
+            def _(k, pair=pair):
+                send_to(turns[pair + 1] * GROUP + w)
 
         pltpu.make_async_copy(
             grid_ref.at[me * slots + slot], here, first_recv.at[slot]
@@ -219,32 +228,18 @@
     loads[0].wait()
     upper = z >= GROUPS // 2
     wait_bytes(got.at[0], first_recv.at[0])
-    far, near, next_far, own = z_mixed
-    analyse(0, far)
-
-    @pl.loop(0, GROUP)
-    def _(k):
-        copy_to(0, far * GROUP + (w + k) % GROUP)
-
-    analyse(0, next_far)
-    analyse(0, near)
-
-    @pl.loop(0, GROUP)
-    def _(k):
-        for there in (next_far, near):
+    for there, skip in zip(turns, skips):
+        analyse(0, there)
+
+        @pl.loop(skip, GROUP)
+        def _(k, there=there):
             copy_to(0, there * GROUP + (w + k) % GROUP)
-
-    analyse(0, own)
-
-    @pl.loop(1, GROUP)
-    def _(k):
-        copy_to(0, own * GROUP + (w + k) % GROUP)
 
     keep_own(0)
     wait_bytes(got.at[1], first_recv.at[1])
     up = z // (GROUPS // 2)
-    one = far + up * (near - far)
-    two = next_far + up * (own - next_far)
+    one = GROUPS - 1 + up * (z_order[2] - (GROUPS - 1))
+    two = GROUPS - 2 + up * (z - (GROUPS - 2))
 
     def copy_half(there, skip, half):
         @pl.loop(skip, GROUP)

time: 123 us -> 122 us (level)
  the two profiles are of different devices: /device:TPU:29 before, /device:TPU:21 now
where the time goes in v5:
time: 122 us
  Pallas kernels  121 us (99%)
  local copies, waits for them, and re-layouts  1.32 us (1%)
    pallas_call x1, Pallas kernels, on_device(): pl.pallas_call(functools.partial(kernel, rows), out_shape=jax.ShapeDtypeS...  121 us

profile of v5, /device:TPU:21, one launch (start us, length us, event | category | flops | bytes accessed | tf_op | source)
XLA Modules:
  0.0 121.9 jit_solution(8857596652236159983)
XLA Ops:
  0.0 120.6 %shard_map.64 = bf16[32,256,128]{2,1,0:T(8,128)(2,1)S(1)} custom-call(s32[2]{0:T(128)} %order_hbm.1, s32[2,2]{1,0:T(2,128)} %boundary_hbm.1, bf16[64,192,128]{2,1,0:T(8,128)(2,1)} %grid_ref.1, bf16[2,1024,1536]{2,1,0:T(8,128)(2,1)} %legendre_ref.1, f32[512,512]{1,0:T(8,128)} %constant.2.clone.table_hbm, bf16[32,256,256]{2,1,0:T(8,128)(2,1)} %inverse_ref.1), custom_call_target="tpu_custom_call" | custom-call | flops 6000000000 | bytes 18874368 | tf_op jit(solution)/shard_map/pallas_call | solution.py:344
  120.6 1.3 %copy.8 = bf16[32,256,128]{2,1,0:T(8,128)(2,1)} copy(bf16[32,256,128]{2,1,0:T(8,128)(2,1)S(1)} %shard_map.64) | data formatting | bytes 4194304

commit v6 on v5

--- a/solution.py
+++ b/solution.py
@@ -138,37 +138,51 @@
 
     pl.semaphore_wait(barrier, devices - 1)
 
-    def to_slots(slot):
+    def to_slots(slot, pair):
         here = got.at[slot, row, pl.ds(pl.multiple_of(ma * band, 16), band)]
 
         def send_to(other):
             pltpu.make_async_remote_copy(
                 src_ref=grid_ref.at[other * slots + slot],
                 dst_ref=here,
-                send_sem=first_send.at[slot],
+                send_sem=first_send.at[slot, pair],
                 recv_sem=first_recv.at[slot],
                 device_id=(other // rows, other % rows),
                 device_id_type=MESH,
             ).start()
 
-        for pair in range(0, 4, 2):
-            @pl.loop(1, GROUP)
-            def _(k, pair=pair):
-                for there in turns[pair:pair + 2]:
-                    send_to(there * GROUP + (w + k) % GROUP)
-
-            send_to(turns[pair] * GROUP + w)
-
-            @pl.loop(skips[pair + 1], 1)
-            def _(k, pair=pair):
-                send_to(turns[pair + 1] * GROUP + w)
-
-        pltpu.make_async_copy(
-            grid_ref.at[me * slots + slot], here, first_recv.at[slot]
-        ).start()
-
-    for slot in range(slots):
-        to_slots(slot)
+        one, two = turns[2 * pair:2 * pair + 2]
+
+        @pl.loop(1, GROUP)
+        def _(k):
+            send_to(one * GROUP + (w + k) % GROUP)
+            send_to(two * GROUP + (w + k) % GROUP)
+
+        send_to(one * GROUP + w)
+
+        @pl.loop(skips[2 * pair + 1], 1)
+        def _(k):
+            send_to(two * GROUP + w)
+
+        if pair == 1:
+            pltpu.make_async_copy(
+                grid_ref.at[me * slots + slot], here, first_recv.at[slot]
+            ).start()
+
+    def wait_bytes(ref, sem):
+        pltpu.make_async_copy(ref, ref, sem).wait()
+
+    def left(slot, pair):
+        own = skips[2 * pair + 1]
+        for less in range(2):
+            @pl.when(own == less)
+            def _(less=less):
+                wait_bytes(
+                    grid_ref.at[pl.ds(0, 2 * GROUP - less)], first_send.at[slot, pair]
+                )
+
+    to_slots(0, 0)
+    to_slots(0, 1)
 
     for load in loads[1:]:
         load.wait()
@@ -222,21 +236,22 @@
         source, here, sem = to_degree(slot, me, half)
         pltpu.make_async_copy(source, here, sem).start()
 
-    def wait_bytes(ref, sem):
-        pltpu.make_async_copy(ref, ref, sem).wait()
+    for pair in range(2):
+        left(0, pair)
+        to_slots(1, pair)
 
     loads[0].wait()
     upper = z >= GROUPS // 2
     wait_bytes(got.at[0], first_recv.at[0])
+    for there in turns:
+        analyse(0, there)
+    wait_bytes(got.at[1], first_recv.at[1])
     for there, skip in zip(turns, skips):
-        analyse(0, there)
-
         @pl.loop(skip, GROUP)
         def _(k, there=there):
             copy_to(0, there * GROUP + (w + k) % GROUP)
 
     keep_own(0)
-    wait_bytes(got.at[1], first_recv.at[1])
     up = z // (GROUPS // 2)
     one = GROUPS - 1 + up * (z_order[2] - (GROUPS - 1))
     two = GROUPS - 2 + up * (z - (GROUPS - 2))
@@ -305,8 +320,8 @@
         done = pl.ds(step * some, some)
         pltpu.make_async_copy(solved.at[done], out_ref.at[done], out_sem).start()
 
-    for slot in range(slots):
-        wait_bytes(grid_ref.at[pl.ds(0, devices - 1)], first_send.at[slot])
+    for pair in range(2):
+        left(1, pair)
     wait_bytes(send.at[0, pl.ds(0, (devices - 1) * share)], second_send.at[0])
 
     @pl.when(upper)
@@ -359,7 +374,7 @@
             pltpu.VMEM((slots, devices, share, full_width), jnp.bfloat16),
             pltpu.VMEM((2, share * orders, width), jnp.float32),
             pltpu.VMEM((share, 2 * width, orders), jnp.bfloat16),
-            dma((5,)), dma((slots,)), dma((slots,)), dma((slots,)), dma((slots, 2, GROUPS)), dma,
+            dma((5,)), dma((slots, 2)), dma((slots,)), dma((slots,)), dma((slots, 2, GROUPS)), dma,
         ],
         compiler_params=pltpu.CompilerParams(
             collective_id=0, has_side_effects=True, vmem_limit_bytes=44 * 2 ** 20

time: 122 us -> 123 us (level)
  the two profiles are of different devices: /device:TPU:21 before, /device:TPU:29 now
where the time goes in v6:
time: 123 us; the launch traced here: 121 us
  Pallas kernels  120 us (98%)
  local copies, waits for them, and re-layouts  1.32 us (1%)
    pallas_call x1, Pallas kernels, on_device(): pl.pallas_call(functools.partial(kernel, rows), out_shape=jax.ShapeDtypeS...  120 us

profile of v6, /device:TPU:29, one launch (start us, length us, event | category | flops | bytes accessed | tf_op | source)
XLA Modules:
  0.0 121.0 jit_solution(1266195227110034258)
XLA Ops:
  0.0 119.7 %shard_map.64 = bf16[32,256,128]{2,1,0:T(8,128)(2,1)S(1)} custom-call(s32[2]{0:T(128)} %order_hbm.1, s32[2,2]{1,0:T(2,128)} %boundary_hbm.1, bf16[64,192,128]{2,1,0:T(8,128)(2,1)} %grid_ref.1, bf16[2,1024,1536]{2,1,0:T(8,128)(2,1)} %legendre_ref.1, f32[512,512]{1,0:T(8,128)} %constant.2.clone.table_hbm, bf16[32,256,256]{2,1,0:T(8,128)(2,1)} %inverse_ref.1), custom_call_target="tpu_custom_call" | custom-call | flops 6000000000 | bytes 18874368 | tf_op jit(solution)/shard_map/pallas_call | solution.py:359
  119.7 1.3 %copy.8 = bf16[32,256,128]{2,1,0:T(8,128)(2,1)} copy(bf16[32,256,128]{2,1,0:T(8,128)(2,1)S(1)} %shard_map.64) | data formatting | bytes 4194304

commit v7 on v5

--- a/solution.py
+++ b/solution.py
@@ -103,7 +103,7 @@
     share = landed.shape[2]
     tile = GROUP * share
     width = stage.shape[2]
-    orders = stage.shape[1] // share
+    orders = 2 * slots * devices
     ma = lax.axis_index("ma")
     row = lax.axis_index("row")
     me = ma * rows + row
@@ -273,7 +273,7 @@
             part = landed.at[slot, pl.ds(source_z * GROUP, GROUP), pl.ds(at, count)]
             wait_bytes(part, second_recv.at[slot, half or 0, source_z])
 
-            @pl.loop(0, GROUP)
+            @pl.loop(0, GROUP, unroll=2)
             def _(k):
                 source = source_z * GROUP + k
                 put(slot, source, at, landed[slot, source, at:at + count].astype(jnp.float32))
@@ -292,7 +292,7 @@
             def _(step=step):
                 gather(1, step // 2)
 
-        @pl.loop(0, some, unroll=4)
+        @pl.loop(0, some, unroll=8)
         def _(k, step=step):
             l = step * some + k
             at = pl.ds(pl.multiple_of(l * orders, orders), orders)
@@ -357,7 +357,7 @@
             pltpu.VMEM((8, full_width), jnp.float32),
             pltpu.VMEM((slots, degrees, full_width), jnp.bfloat16),
             pltpu.VMEM((slots, devices, share, full_width), jnp.bfloat16),
-            pltpu.VMEM((2, share * orders, width), jnp.float32),
+            pltpu.VMEM((2, (share + 1) * orders, width), jnp.float32),
             pltpu.VMEM((share, 2 * width, orders), jnp.bfloat16),
             dma((5,)), dma((slots,)), dma((slots,)), dma((slots,)), dma((slots, 2, GROUPS)), dma,
         ],

time: 122 us -> 122 us (level)
  no operation moved by 1% of the time
where the time goes in v7:
time: 122 us
  Pallas kernels  120 us (98%)
  local copies, waits for them, and re-layouts  1.32 us (1%)
    pallas_call x1, Pallas kernels, on_device(): pl.pallas_call(functools.partial(kernel, rows), out_shape=jax.ShapeDtypeS...  120 us

profile of v7, /device:TPU:21, one launch (start us, length us, event | category | flops | bytes accessed | tf_op | source)
XLA Modules:
  0.0 121.6 jit_solution(4171858646714196015)
XLA Ops:
  0.0 120.3 %shard_map.64 = bf16[32,256,128]{2,1,0:T(8,128)(2,1)S(1)} custom-call(s32[2]{0:T(128)} %order_hbm.1, s32[2,2]{1,0:T(2,128)} %boundary_hbm.1, bf16[64,192,128]{2,1,0:T(8,128)(2,1)} %grid_ref.1, bf16[2,1024,1536]{2,1,0:T(8,128)(2,1)} %legendre_ref.1, f32[512,512]{1,0:T(8,128)} %constant.2.clone.table_hbm, bf16[32,256,256]{2,1,0:T(8,128)(2,1)} %inverse_ref.1), custom_call_target="tpu_custom_call" | custom-call | flops 6000000000 | bytes 18874368 | tf_op jit(solution)/shard_map/pallas_call | solution.py:344
  120.3 1.3 %copy.8 = bf16[32,256,128]{2,1,0:T(8,128)(2,1)} copy(bf16[32,256,128]{2,1,0:T(8,128)(2,1)S(1)} %shard_map.64) | data formatting | bytes 4194304
